TPU v7x, 32 devices: a whole 2x2x4 slice. The times are simulated.
32 devices in a mesh: groups: 2 (over x), blk: 16 (over z, y, core).
Axes of the slice: x: 2, y: 2, z: 4, core: 2. Of those that a mesh axis runs over, the one named last changes fastest.
Arguments:
- ocean_fields: float32 [8, 2048, 8, 128], P(None, ('groups', 'blk')), parts along dimension 1, may hold values from -1.5 to 8, as said below
- stress_in: float32 [3, 256, 4096], P(None, ('groups', 'blk')), parts along dimension 1, may hold values from -3 to 3
- ocean_slot: int32 [512], replicated, may hold values from 0 to 1023, as said below
- ice_mask: int32 [512], replicated, may hold values 0 or 1
Outputs:
- velocity_out: float32 [2, 2048, 8, 128], P(None, ('groups', 'blk')), parts along dimension 1
- stress_out: float32 [3, 256, 4096], P(None, ('groups', 'blk')), parts along dimension 1
There are 2 independent parts, one for each index of `groups`. A program takes and returns all parts, laid end to end along the dimension named above; an argument that names none is the same for every part. Nothing has to cross between parts.
Inputs may be any that keep to these rules, and one draw needn't show every extreme that they name: Entries are distinct. Ice block i lies in slot ocean_slot[i] % 64 of ocean owner ocean_slot[i] // 64. Among the 32 ice blocks sharing i // 32, each ocean owner holds none or exactly 4; ocean owner 16 - 1 holds 64 ice blocks in all, one in each of its slots. `ocean_fields`: fields 0, 1, 4, 5, 6, 7 lie within -1.5 to 1.5; field 2 within 0.1 to 8; field 3 within 0.5 to 4.
All inputs are finite; a program needn't handle non-finite values.
Results may differ from a plain program's by a relative error of at most 0.000033.
Values sent between devices are 32-bit elements; how exact they have to be, the bound alone decides.
A program may use at most 64 MiB of HBM per device.

v0:
```python
import jax
import jax.numpy as jnp
from jax import lax
from jax.sharding import PartitionSpec as P

ITERS = 6


EINV_SQ = 0.25
DELTA_MIN_SQ = 0.01
RELAXATION = 1.0
INV_STEP = 1.0
DRAG_COEFF = 0.5
CORIOLIS = 0.5
SPEED_MIN_SQ = 0.0025


def extended_2(block, sides, width):
    for axis, dim in sides:
        count = lax.axis_size(axis)
        forward = [(i, i + 1) for i in range(count - 1)]
        backward = [(target, source) for source, target in forward]
        low = lax.ppermute(
            lax.slice_in_dim(block, block.shape[dim] - width, None, axis=dim), axis, forward
        )
        high = lax.ppermute(lax.slice_in_dim(block, 0, width, axis=dim), axis, backward)
        block = jnp.concatenate([low, block, high], axis=dim)
    return block


def column_next(values):
    return jnp.roll(values, -1, axis=1)


def column_prev(values):
    return jnp.roll(values, 1, axis=1)


def rolled_next(values):
    return jnp.roll(values, -1, axis=0)


def rolled_prev(values):
    return jnp.roll(values, 1, axis=0)


def stress_section(
    vel_x, vel_y, stress_p, stress_m, stress_xy, strength, live_mask, row_next, row_prev
):
    grad_ux = 0.5 * (column_next(vel_x) - column_prev(vel_x))
    grad_vy = 0.5 * (row_next(vel_y) - row_prev(vel_y))
    grad_uy = 0.5 * (row_next(vel_x) - row_prev(vel_x))
    grad_vx = 0.5 * (column_next(vel_y) - column_prev(vel_y))
    divergence = grad_ux + grad_vy
    tension = grad_ux - grad_vy
    shear_rate = grad_uy + grad_vx
    delta_rate = jnp.sqrt(
        divergence * divergence
        + (tension * tension + shear_rate * shear_rate) * EINV_SQ
        + DELTA_MIN_SQ
    )
    scaled = RELAXATION * strength / delta_rate
    new_p = live_mask * (stress_p + scaled * (divergence - delta_rate)) / (1.0 + RELAXATION)
    new_m = live_mask * (stress_m + scaled * tension * EINV_SQ) / (1.0 + RELAXATION)
    new_xy = live_mask * (stress_xy + scaled * shear_rate * (0.5 * EINV_SQ)) / (1.0 + RELAXATION)
    return (new_p, new_m, new_xy)


def momentum_section(
    vel_x,
    vel_y,
    stress_p,
    stress_m,
    stress_xy,
    ice_mass,
    wind_x,
    wind_y,
    current_x,
    current_y,
    cell_mask,
    row_valid,
    row_next,
    row_prev,
):
    normal_xx = 0.5 * (stress_p + stress_m)
    normal_yy = 0.5 * (stress_p - stress_m)
    force_x = 0.5 * (column_next(normal_xx) - column_prev(normal_xx)) + 0.5 * (
        row_next(stress_xy) - row_prev(stress_xy)
    )
    force_y = 0.5 * (column_next(stress_xy) - column_prev(stress_xy)) + 0.5 * (
        row_next(normal_yy) - row_prev(normal_yy)
    )
    rel_x = vel_x - current_x
    rel_y = vel_y - current_y
    drag_rate = DRAG_COEFF * jnp.sqrt(rel_x * rel_x + rel_y * rel_y + SPEED_MIN_SQ)
    inertia = ice_mass * INV_STEP
    diagonal = inertia + drag_rate
    turning = CORIOLIS * ice_mass
    rhs_x = inertia * vel_x + force_x + wind_x + drag_rate * current_x
    rhs_y = inertia * vel_y + force_y + wind_y + drag_rate * current_y
    determinant = diagonal * diagonal + turning * turning
    solved_x = (diagonal * rhs_x + turning * rhs_y) / determinant
    solved_y = (diagonal * rhs_y - turning * rhs_x) / determinant
    new_x = (cell_mask * solved_x + (1.0 - cell_mask) * current_x) * row_valid
    new_y = (cell_mask * solved_y + (1.0 - cell_mask) * current_y) * row_valid
    return (new_x, new_y)


def run_cycle(fields_now, coeffs, cell_mask, row_valid):
    new_p, new_m, new_xy = stress_section(
        fields_now[0],
        fields_now[1],
        fields_now[2],
        fields_now[3],
        fields_now[4],
        coeffs[0],
        cell_mask * row_valid,
        rolled_next,
        rolled_prev,
    )
    new_x, new_y = momentum_section(
        fields_now[0],
        fields_now[1],
        new_p,
        new_m,
        new_xy,
        coeffs[1],
        coeffs[2],
        coeffs[3],
        coeffs[4],
        coeffs[5],
        cell_mask,
        row_valid,
        rolled_next,
        rolled_prev,
    )
    return jnp.stack([new_x, new_y, new_p, new_m, new_xy])


def per_device(ocean_fields, stress_in, ocean_slot, ice_mask):
    owners = lax.axis_size("blk")
    my_index = lax.axis_index("blk")
    field_count, slot_count, block_rows, block_cols = ocean_fields.shape
    strip_cols = stress_in.shape[2]
    per_owner = strip_cols // block_cols
    pair_cap = 2 * per_owner // owners
    source = ocean_slot // slot_count
    slot_place = ocean_slot % slot_count
    source_grid = source.reshape(owners, per_owner)
    earlier = jnp.arange(per_owner)[None, :] < jnp.arange(per_owner)[:, None]
    same_owner = source_grid[:, :, None] == source_grid[:, None, :]
    pair_rank = jnp.sum(jnp.where(same_owner & earlier[None], 1, 0), axis=2).astype(jnp.int32)
    dest_grid = jnp.broadcast_to(jnp.arange(owners, dtype=jnp.int32)[:, None], (owners, per_owner))
    position = (dest_grid * pair_cap + pair_rank).reshape(-1)
    is_mine = source == my_index
    buffer_slots = owners * pair_cap
    send_index = (
        jnp.full((buffer_slots,), slot_count, jnp.int32)
        .at[jnp.where(is_mine, position, buffer_slots)]
        .set(slot_place, mode="drop")
    )
    padded = jnp.concatenate(
        [ocean_fields, jnp.zeros((field_count, 1, block_rows, block_cols), ocean_fields.dtype)],
        axis=1,
    )
    outgoing = jnp.take(padded, send_index, axis=1)
    incoming = lax.all_to_all(outgoing, "blk", split_axis=1, concat_axis=1, tiled=True)
    my_source = lax.dynamic_slice_in_dim(source_grid, my_index, 1, 0)[0]
    my_rank = lax.dynamic_slice_in_dim(pair_rank, my_index, 1, 0)[0]
    receive_index = my_source * pair_cap + my_rank
    my_blocks = jnp.take(incoming, receive_index, axis=1)
    ice_strip = my_blocks.transpose(0, 2, 1, 3).reshape(field_count, block_rows, strip_cols)
    rim_depth = 4
    coeffs = extended_2(ice_strip[2:], (("blk", 1),), rim_depth)
    ext_rows = block_rows + 2 * rim_depth
    global_row = my_index * block_rows + jnp.arange(ext_rows, dtype=jnp.int32) - rim_depth
    row_valid = ((global_row >= 0) & (global_row < owners * block_rows)).astype(jnp.float32)[
        :, None
    ]
    owner_row = jnp.clip(global_row // block_rows, 0, owners - 1)
    mask_grid = ice_mask.reshape(owners, per_owner).astype(jnp.float32)
    block_mask = jnp.take(mask_grid, owner_row, axis=0)
    cell_mask = jnp.broadcast_to(block_mask[:, :, None], (ext_rows, per_owner, block_cols)).reshape(
        ext_rows, strip_cols
    )
    fields_now = jnp.concatenate([ice_strip[0:2], stress_in], axis=0)
    for pair_index in range(ITERS // 2):
        extended = extended_2(fields_now, (("blk", 1),), rim_depth)
        extended = run_cycle(extended, coeffs, cell_mask, row_valid)
        extended = run_cycle(extended, coeffs, cell_mask, row_valid)
        fields_now = extended[:, rim_depth : rim_depth + block_rows]
    velocity_blocks = (
        fields_now[0:2].reshape(2, block_rows, per_owner, block_cols).transpose(0, 2, 1, 3)
    )
    back_send = (
        jnp.zeros((2, buffer_slots, block_rows, block_cols), jnp.float32)
        .at[:, receive_index]
        .set(velocity_blocks)
    )
    back_home = lax.all_to_all(back_send, "blk", split_axis=1, concat_axis=1, tiled=True)
    velocity_out = (
        jnp.zeros((2, slot_count + 1, block_rows, block_cols), jnp.float32)
        .at[:, send_index]
        .set(back_home)[:, :slot_count]
    )
    return (velocity_out, fields_now[2:5])


def solution(mesh):
    placed = (P(None, ("groups", "blk"), None, None), P(None, ("groups", "blk"), None), P(), P())
    return jax.shard_map(
        per_device,
        mesh=mesh,
        in_specs=placed,
        out_specs=(P(None, ("groups", "blk"), None, None), P(None, ("groups", "blk"), None)),
        check_vma=False,
    )
```

profile of v0, /device:TPU:0, one launch (start us, length us, event | category | flops | bytes accessed | tf_op | source)
XLA Modules:
  0.0 168.6 jit_solution(1224905214965595038)
XLA Ops:
  0.7 0.7 add_select_fusion
  1.4 0.5 select_reduce_fusion
  2.1 2.4 %scatter_custom_fusion = s32[64]{0:T(128)S(1)} fusion(s32[512]{0:T(512)S(1)} %compare_select_fusion, s32[512]{0:T(512)S(1)} %get-tuple-element.452, s32[]{:T(128)} %constant.118.clone.1), kind=kCustom, calls=%fused_computation.510 | custom fusion | bytes 260 | tf_op jit(solution)/shard_map/scatter | solution.py:160
  4.5 1.7 %concatenate.1944 = f32[8,65,8,128]{3,2,1,0:T(8,128)S(1)} pad(f32[8,64,8,128]{3,2,1,0:T(8,128)} %param.4, f32[]{:T(128)} %constant.117.clone.1), padding=0_0x0_1x0_0x0_0 | pad | bytes 4227076 | tf_op jit(solution)/shard_map/concatenate | solution.py:162
  6.3 2.0 %gather_fusion.1 = f32[64,8,8,128]{3,2,1,0:T(8,128)} fusion(f32[8,65,8,128]{3,2,1,0:T(8,128)S(1)} %concatenate.1944, s32[1024]{0:T(1024)S(1)} %pad_clamp_fusion.1), kind=kCustom, calls=%fused_computation.1 | custom fusion | bytes 4194560 | tf_op jit(solution)/shard_map/jit(_take)/gather | solution.py:166
  8.3 3.1 %select_bitcast_fusion = f32[8,64,8,128]{3,2,0,1:T(8,128)} fusion(f32[64,8,8,128]{3,2,1,0:T(8,128)} %gather_fusion.1, pred[64]{0:T(512)(128)(4,1)S(1)} %compare_and_fusion), kind=kLoop, calls=%fused_computation.6 | loop fusion | flops 524288 | bytes 4194368 | tf_op jit(solution)/shard_map/jit(_take)/select_n | solution.py:166
  11.4 7.5 %all-to-all-start = ((f32[8,64,8,128]{3,2,0,1:T(8,128)}), f32[8,64,8,128]{3,2,0,1:T(8,128)S(1)}, u32[]{:S(2)}, u32[]{:S(2)}) async-start(f32[8,64,8,128]{3,2,0,1:T(8,128)} %select_bitcast_fusion), calls=%async_computation | async-start | bytes 4194304 | tf_op jit(solution)/shard_map/all_to_all | solution.py:167
  19.1 0.6 gather_fusion
  19.9 40.1 %all-to-all-done = f32[8,64,8,128]{3,2,0,1:T(8,128)S(1)} async-done(((f32[8,64,8,128]{3,2,0,1:T(8,128)}), f32[8,64,8,128]{3,2,0,1:T(8,128)S(1)}, u32[]{:S(2)}, u32[]{:S(2)}) %all-to-all-start) | async-done | bytes 2097184 | tf_op jit(solution)/shard_map/all_to_all | solution.py:167
  60.0 1.6 gather_fusion.2
  61.6 1.4 select_bitcast_fusion.1
  63.1 0.9 copy-done
  64.1 2.7 %collective-permute-start.2 = (f32[5,4,4096]{2,1,0:T(4,128)S(1)}, f32[5,4,4096]{2,1,0:T(4,128)S(1)}, u32[]{:S(2)}, u32[]{:S(2)}) collective-permute-start(f32[5,4,4096]{2,1,0:T(4,128)S(1)} %get-tuple-element.138), channel_id=1, source_target_pairs={{0,1},{1,2},{2,3},{3,4},{4,5},{5,6},{6,7},{7,8},{8,9},{9,10},{10,1... | collective-permute-start | bytes 983048 | tf_op jit(solution)/shard_map/ppermute | solution.py:23
  66.8 1.3 collective-permute-start.3
  68.2 5.3 %collective-permute-start = (f32[6,4,4096]{2,1,0:T(4,128)S(1)}, f32[6,4,4096]{2,1,0:T(4,128)S(1)}, u32[]{:S(2)}, u32[]{:S(2)}) collective-permute-start(f32[6,4,4096]{2,1,0:T(4,128)S(1)} %get-tuple-element.136), channel_id=1, source_target_pairs={{0,1},{1,2},{2,3},{3,4},{4,5},{5,6},{6,7},{7,8},{8,9},{9,10},{10,1... | collective-permute-start | bytes 1179656 | tf_op jit(solution)/shard_map/ppermute | solution.py:23
  73.5 1.3 collective-permute-start.1
  75.7 2.5 %collective-permute-done.1 = f32[6,4,4096]{2,1,0:T(4,128)S(1)} collective-permute-done((f32[6,4,4096]{2,1,0:T(4,128)S(1)}, f32[6,4,4096]{2,1,0:T(4,128)S(1)}, u32[]{:S(2)}, u32[]{:S(2)}) %collective-permute-start.1) | collective-permute-done | bytes 393248 | tf_op jit(solution)/shard_map/ppermute | solution.py:26
  78.3 0.3 pad_maximum_fusion
  78.6 0.6 add_multiply_fusion.13
  79.2 0.3 fusion.184
  80.2 0.7 fusion.4
  81.0 0.3 fusion.2
  81.9 0.6 add_multiply_fusion.10
  82.5 0.3 multiply_multiply_fusion.9
  83.5 0.6 add_multiply_fusion.12
  84.1 0.7 multiply_dynamic-update-slice_fusion.9
  85.0 0.9 multiply_dynamic-update-slice_fusion.7
  85.9 0.3 multiply_dynamic-update-slice_fusion.6
  86.2 0.3 multiply_dynamic-update-slice_fusion.5
  86.6 9.3 %collective-permute-start.4 = (f32[5,4,4096]{2,1,0:T(4,128)S(1)}, f32[5,4,4096]{2,1,0:T(4,128)S(1)}, u32[]{:S(2)}, u32[]{:S(2)}) collective-permute-start(f32[5,4,4096]{2,1,0:T(4,128)S(1)} %get-tuple-element.124), channel_id=1, source_target_pairs={{0,1},{1,2},{2,3},{3,4},{4,5},{5,6},{6,7},{7,8},{8,9},{9,10},{10,1... | collective-permute-start | bytes 983048 | tf_op jit(solution)/shard_map/ppermute | solution.py:23
  96.0 1.5 collective-permute-start.5
  97.5 2.0 %collective-permute-done.5 = f32[5,4,4096]{2,1,0:T(4,128)S(1)} collective-permute-done((f32[5,4,4096]{2,1,0:T(4,128)S(1)}, f32[5,4,4096]{2,1,0:T(4,128)S(1)}, u32[]{:S(2)}, u32[]{:S(2)}) %collective-permute-start.5) | collective-permute-done | bytes 327712 | tf_op jit(solution)/shard_map/ppermute | solution.py:26
  99.5 0.2 pad_maximum_fusion.2
  100.5 0.6 add_multiply_fusion.9
  101.1 0.3 fusion.159
  102.2 0.7 fusion.8
  102.9 0.3 fusion.6
  103.8 0.6 add_multiply_fusion.6
  104.4 0.3 multiply_multiply_fusion.6
  105.4 0.6 add_multiply_fusion.8
  106.0 0.7 multiply_dynamic-update-slice_fusion.4
  106.9 0.9 multiply_dynamic-update-slice_fusion.2
  107.8 0.3 multiply_dynamic-update-slice_fusion.1
  108.1 0.3 multiply_dynamic-update-slice_fusion
  108.8 1.3 collective-permute-start.7
  110.1 11.2 %collective-permute-start.6 = (f32[5,4,4096]{2,1,0:T(4,128)S(1)}, f32[5,4,4096]{2,1,0:T(4,128)S(1)}, u32[]{:S(2)}, u32[]{:S(2)}) collective-permute-start(f32[5,4,4096]{2,1,0:T(4,128)S(1)} %get-tuple-element.112), channel_id=1, source_target_pairs={{0,1},{1,2},{2,3},{3,4},{4,5},{5,6},{6,7},{7,8},{8,9},{9,10},{10,1... | collective-permute-start | bytes 983048 | tf_op jit(solution)/shard_map/ppermute | solution.py:23
  121.6 0.7 collective-permute-done.6
  123.2 0.6 add_multiply_fusion.5
  123.8 0.3 fusion.153
  124.9 0.7 fusion.12
  125.6 0.3 fusion.10
  126.5 0.6 subtract_multiply_fusion
  127.2 0.3 multiply_multiply_fusion.3
  128.1 0.6 add_multiply_fusion.4
  128.7 0.9 multiply_multiply_fusion.2
  129.6 0.5 multiply_multiply_fusion.1
  130.1 0.6 add_multiply_fusion.1
  131.0 1.9 %scatter_fusion = f32[2,64,8,128]{3,2,1,0:T(8,128)S(1)} fusion(f32[2,64,8,128]{3,2,1,0:T(8,128)S(1)} %broadcast_in_dim.80, s32[32]{0:T(128)S(1)} %fusion.190, f32[32,2,8,128]{3,2,1,0:T(8,128)S(1)} %copy_bitcast_fusion.1), kind=kCustom, calls=%fused_computation.4 | custom fusion | bytes 786560 | tf_op jit(solution)/shard_map/scatter | solution.py:198
  132.9 0.8 copy.378
  133.7 16.7 %all-to-all-start.1 = ((f32[2,64,8,128]{3,2,0,1:T(8,128)}), f32[2,64,8,128]{3,2,0,1:T(8,128)S(1)}, u32[]{:S(2)}, u32[]{:S(2)}) async-start(f32[2,64,8,128]{3,2,0,1:T(8,128)} %copy.378), calls=%async_computation.1 | async-start | bytes 1048576 | tf_op jit(solution)/shard_map/all_to_all | solution.py:200
  150.4 0.8 pad_maximum_fusion.4
  151.2 13.7 %all-to-all-done.1 = f32[2,64,8,128]{3,2,0,1:T(8,128)S(1)} async-done(((f32[2,64,8,128]{3,2,0,1:T(8,128)}), f32[2,64,8,128]{3,2,0,1:T(8,128)S(1)}, u32[]{:S(2)}, u32[]{:S(2)}) %all-to-all-start.1) | async-done | bytes 524320 | tf_op jit(solution)/shard_map/all_to_all | solution.py:200
  164.9 2.8 %scatter_fusion.1 = f32[2,65,8,128]{3,2,1,0:T(8,128)S(1)} fusion(f32[2,65,8,128]{3,2,1,0:T(8,128)S(1)} %broadcast_in_dim.73, s32[64]{0:T(128)S(1)} %compare_select_fusion.5, f32[64,2,8,128]{3,2,1,0:T(8,128)S(1)} %bitcast.843), kind=kCustom, calls=%fused_computation.5 | custom fusion | bytes 1573120 | tf_op jit(solution)/shard_map/scatter | solution.py:204
  167.7 0.8 slice.1336
  (148 shorter events, 10.5 us)
Async XLA Ops:
  11.4 7.5 %copy-start.1 = (s32[512]{0:T(512)S(1)}, s32[512]{0:T(512)}, u32[]{:S(2)}) copy-start(s32[512]{0:T(512)} %param.7) | copy-start | bytes 6148
  11.4 48.6 %all-to-all-start = ((f32[8,64,8,128]{3,2,0,1:T(8,128)}), f32[8,64,8,128]{3,2,0,1:T(8,128)S(1)}, u32[]{:S(2)}, u32[]{:S(2)}) async-start(f32[8,64,8,128]{3,2,0,1:T(8,128)} %select_bitcast_fusion), calls=%async_computation | async-start | bytes 4194304 | tf_op jit(solution)/shard_map/all_to_all | solution.py:167
  63.0 1.0 copy-start
  64.1 10.7 %collective-permute-start.2 = (f32[5,4,4096]{2,1,0:T(4,128)S(1)}, f32[5,4,4096]{2,1,0:T(4,128)S(1)}, u32[]{:S(2)}, u32[]{:S(2)}) collective-permute-start(f32[5,4,4096]{2,1,0:T(4,128)S(1)} %get-tuple-element.138), channel_id=1, source_target_pairs={{0,1},{1,2},{2,3},{3,4},{4,5},{5,6},{6,7},{7,8},{8,9},{9,10},{10,1... | collective-permute-start | bytes 983048 | tf_op jit(solution)/shard_map/ppermute | solution.py:23
  66.8 8.0 %collective-permute-start.3 = (f32[5,4,4096]{2,1,0:T(4,128)S(1)}, f32[5,4,4096]{2,1,0:T(4,128)S(1)}, u32[]{:S(2)}, u32[]{:S(2)}) collective-permute-start(f32[5,4,4096]{2,1,0:T(4,128)S(1)} %get-tuple-element.139), channel_id=1, source_target_pairs={{1,0},{2,1},{3,2},{4,3},{5,4},{6,5},{7,6},{8,7},{9,8},{10,9},{11,1... | collective-permute-start | bytes 983048 | tf_op jit(solution)/shard_map/ppermute | solution.py:26
  68.2 7.6 %collective-permute-start = (f32[6,4,4096]{2,1,0:T(4,128)S(1)}, f32[6,4,4096]{2,1,0:T(4,128)S(1)}, u32[]{:S(2)}, u32[]{:S(2)}) collective-permute-start(f32[6,4,4096]{2,1,0:T(4,128)S(1)} %get-tuple-element.136), channel_id=1, source_target_pairs={{0,1},{1,2},{2,3},{3,4},{4,5},{5,6},{6,7},{7,8},{8,9},{9,10},{10,1... | collective-permute-start | bytes 1179656 | tf_op jit(solution)/shard_map/ppermute | solution.py:23
  73.5 4.8 %collective-permute-start.1 = (f32[6,4,4096]{2,1,0:T(4,128)S(1)}, f32[6,4,4096]{2,1,0:T(4,128)S(1)}, u32[]{:S(2)}, u32[]{:S(2)}) collective-permute-start(f32[6,4,4096]{2,1,0:T(4,128)S(1)} %get-tuple-element.137), channel_id=1, source_target_pairs={{1,0},{2,1},{3,2},{4,3},{5,4},{6,5},{7,6},{8,7},{9,8},{10,9},{11,1... | collective-permute-start | bytes 1179656 | tf_op jit(solution)/shard_map/ppermute | solution.py:26
  86.6 10.9 %collective-permute-start.4 = (f32[5,4,4096]{2,1,0:T(4,128)S(1)}, f32[5,4,4096]{2,1,0:T(4,128)S(1)}, u32[]{:S(2)}, u32[]{:S(2)}) collective-permute-start(f32[5,4,4096]{2,1,0:T(4,128)S(1)} %get-tuple-element.124), channel_id=1, source_target_pairs={{0,1},{1,2},{2,3},{3,4},{4,5},{5,6},{6,7},{7,8},{8,9},{9,10},{10,1... | collective-permute-start | bytes 983048 | tf_op jit(solution)/shard_map/ppermute | solution.py:23
  96.0 3.5 %collective-permute-start.5 = (f32[5,4,4096]{2,1,0:T(4,128)S(1)}, f32[5,4,4096]{2,1,0:T(4,128)S(1)}, u32[]{:S(2)}, u32[]{:S(2)}) collective-permute-start(f32[5,4,4096]{2,1,0:T(4,128)S(1)} %get-tuple-element.125), channel_id=1, source_target_pairs={{1,0},{2,1},{3,2},{4,3},{5,4},{6,5},{7,6},{8,7},{9,8},{10,9},{11,1... | collective-permute-start | bytes 983048 | tf_op jit(solution)/shard_map/ppermute | solution.py:26
  108.8 12.5 %collective-permute-start.7 = (f32[5,4,4096]{2,0,1:T(8,128)S(1)}, f32[5,4,4096]{2,0,1:T(8,128)S(1)}, u32[]{:S(2)}, u32[]{:S(2)}) collective-permute-start(f32[5,4,4096]{2,0,1:T(8,128)S(1)} %copy.365), channel_id=1, source_target_pairs={{1,0},{2,1},{3,2},{4,3},{5,4},{6,5},{7,6},{8,7},{9,8},{10,9},{11,1... | collective-permute-start | bytes 983048 | tf_op jit(solution)/shard_map/ppermute | solution.py:26
  110.1 12.2 %collective-permute-start.6 = (f32[5,4,4096]{2,1,0:T(4,128)S(1)}, f32[5,4,4096]{2,1,0:T(4,128)S(1)}, u32[]{:S(2)}, u32[]{:S(2)}) collective-permute-start(f32[5,4,4096]{2,1,0:T(4,128)S(1)} %get-tuple-element.112), channel_id=1, source_target_pairs={{0,1},{1,2},{2,3},{3,4},{4,5},{5,6},{6,7},{7,8},{8,9},{9,10},{10,1... | collective-permute-start | bytes 983048 | tf_op jit(solution)/shard_map/ppermute | solution.py:23
  133.7 31.2 %all-to-all-start.1 = ((f32[2,64,8,128]{3,2,0,1:T(8,128)}), f32[2,64,8,128]{3,2,0,1:T(8,128)S(1)}, u32[]{:S(2)}, u32[]{:S(2)}) async-start(f32[2,64,8,128]{3,2,0,1:T(8,128)} %copy.378), calls=%async_computation.1 | async-start | bytes 1048576 | tf_op jit(solution)/shard_map/all_to_all | solution.py:200
where the time goes:
time: 169 us
  waiting for transfers between devices  59 us (35%)
  starting transfers between devices  58 us (34%)
  other arithmetic  25.5 us (15%)
  local copies, waits for them, and re-layouts  24.4 us (14%)
    all_to_all x1, waiting for transfers between devices, per_device(): lax.all_to_all(outgoing, 'blk', split_axis=1, concat_axis=1, tiled=True)  40.1 us
    ppermute x4, starting transfers between devices, extended_2(): lax.ppermute(lax.slice_in_dim(block, block.shape[dim] - width, None, axis...  28.5 us
    all_to_all x1, starting transfers between devices, per_device(): lax.all_to_all(back_send, 'blk', split_axis=1, concat_axis=1, tiled=True)  16.7 us
    all_to_all x1, waiting for transfers between devices, per_device(): lax.all_to_all(back_send, 'blk', split_axis=1, concat_axis=1, tiled=True)  13.7 us
    all_to_all x1, starting transfers between devices, per_device(): lax.all_to_all(outgoing, 'blk', split_axis=1, concat_axis=1, tiled=True)  7.52 us
    ppermute x4, starting transfers between devices, extended_2(): lax.ppermute(lax.slice_in_dim(block, 0, width, axis=dim), axis, backward)  5.35 us
    concatenate x48, local copies, waits for them, and re-layouts, column_next(): return jnp.roll(values, -1, axis=1)  5 us
    ppermute x4, waiting for transfers between devices, extended_2(): lax.ppermute(lax.slice_in_dim(block, 0, width, axis=dim), axis, backward)  4.5 us
  transfers between devices with their start and end apart: 10, of which 5 were waited for; matrix products, arithmetic and copies ran while one was open for 2% of the time, Pallas kernels for 0%

commit v1 on v0

v1 whole, which is shorter than its diff:
```python
import functools

import jax
import jax.numpy as jnp
from jax import lax
from jax.experimental import pallas as pl
from jax.experimental.pallas import tpu as pltpu
from jax.sharding import PartitionSpec as P

ITERS = 6
EINV_SQ = 0.25
DELTA_MIN_SQ = 0.01
DRAG_COEFF = 0.5
CORIOLIS = 0.5
SPEED_MIN_SQ = 0.0025


def index_tables(ocean_slot, owners, slot_count, per_owner, pair_cap, my_index):
    source = (ocean_slot // slot_count).reshape(owners, per_owner)
    place = (ocean_slot % slot_count).reshape(owners, per_owner)
    buffer_slots = owners * pair_cap
    earlier = jnp.arange(per_owner)[None, :] < jnp.arange(per_owner)[:, None]
    is_mine = source == my_index
    rank = jnp.sum(jnp.where(is_mine[:, None, :] & earlier[None], 1, 0), axis=2)
    hit = is_mine[:, :, None] & (rank[:, :, None] == jnp.arange(pair_cap)[None, None, :])
    send_index = (jnp.sum(jnp.where(hit, place[:, :, None] + 1, 0), axis=1) - 1).reshape(-1)
    slots = jnp.arange(slot_count)
    match = send_index[None, :] == slots[:, None]
    home_index = jnp.sum(jnp.where(match, jnp.arange(buffer_slots)[None, :] + 1, 0), axis=1) - 1
    mine = lax.dynamic_slice_in_dim(source, my_index, 1, 0)[0]
    my_rank = jnp.sum(jnp.where((mine[None, :] == mine[:, None]) & earlier, 1, 0), axis=1)
    receive_index = mine * pair_cap + my_rank
    back = receive_index[None, :] == jnp.arange(buffer_slots)[:, None]
    back_index = jnp.sum(jnp.where(back, jnp.arange(per_owner)[None, :], 0), axis=1)
    return jnp.concatenate(
        [jnp.maximum(send_index, 0), home_index, receive_index, back_index]
    ).astype(jnp.int32)


def kernel(
    owners, pair_cap, per_owner, slot_count,
    table, mask_ref, ocean, stress_in, vel_out, stress_out,
    send_buf, recv_buf, back_buf, home_buf, coef, vel, vel_blocks, mask_buf, edge, rim_send, rim_recv,
    send_sem, recv_sem, back_send_sem, back_recv_sem, rim_send_sem, rim_recv_sem,
):
    me = lax.axis_index("blk")
    cap = pair_cap
    positions = owners * cap
    home_at = positions
    receive_at = home_at + slot_count
    back_at = receive_at + per_owner
    cols = stress_in.shape[2]

    rim_recv[...] = jnp.zeros_like(rim_recv)
    barrier = pltpu.get_barrier_semaphore()

    def greet(k, _):
        pl.semaphore_signal(
            barrier, inc=1, device_id={"blk": lax.rem(me + k, owners)},
            device_id_type=pl.DeviceIdType.MESH,
        )
        return 0

    lax.fori_loop(1, owners, greet, 0)
    pl.semaphore_wait(barrier, owners - 1)

    def out_copy(peer):
        return pltpu.make_async_remote_copy(
            src_ref=send_buf.at[pl.ds(peer * cap, cap)],
            dst_ref=recv_buf.at[pl.ds(me * cap, cap)],
            send_sem=send_sem.at[peer],
            recv_sem=recv_sem.at[me],
            device_id={"blk": peer},
            device_id_type=pl.DeviceIdType.MESH,
        )

    def in_copy(peer):
        return pltpu.make_async_remote_copy(
            src_ref=send_buf.at[pl.ds(me * cap, cap)],
            dst_ref=recv_buf.at[pl.ds(peer * cap, cap)],
            send_sem=send_sem.at[me],
            recv_sem=recv_sem.at[peer],
            device_id={"blk": peer},
            device_id_type=pl.DeviceIdType.MESH,
        )

    def send_to(k, _):
        peer = lax.rem(me + k, owners)
        for r in range(cap):
            at = peer * cap + r
            send_buf[at] = ocean[:, table[at]]
        out_copy(peer).start()
        return 0

    half = owners // 2
    lax.fori_loop(half, owners, send_to, 0)
    lax.fori_loop(1, half, send_to, 0)
    for r in range(cap):
        at = me * cap + r
        recv_buf[at] = ocean[:, table[at]]

    row = lax.broadcasted_iota(jnp.int32, (8, 128), 0)
    above = lax.max(me - 1, 0)
    below = lax.min(me + 1, owners - 1)
    above_ok = jnp.where(me > 0, 1.0, 0.0)
    below_ok = jnp.where(me < owners - 1, 1.0, 0.0)

    def mask_block(j, _):
        at = pl.ds(pl.multiple_of(j * 128, 128), 128)
        mask_buf[0, :, at] = jnp.full((8, 128), mask_ref[me * per_owner + j].astype(jnp.float32))
        low = mask_ref[below * per_owner + j].astype(jnp.float32) * below_ok
        high = mask_ref[above * per_owner + j].astype(jnp.float32) * above_ok
        mask_buf[1, :, at] = jnp.where(row < 4, low, high)
        return 0

    lax.fori_loop(0, per_owner, mask_block, 0)
    stress_out[...] = stress_in[...]

    def arrived(k, _):
        in_copy(lax.rem(me + k, owners)).wait_recv()
        return 0

    lax.fori_loop(1, owners, arrived, 0)

    def unpack(j, _):
        at = pl.ds(pl.multiple_of(j * 128, 128), 128)
        block = recv_buf[table[receive_at + j]]
        vel[0, :, at] = block[0]
        vel[1, :, at] = block[1]
        for f in range(6):
            coef[f, :, at] = block[2 + f]
        return 0

    lax.fori_loop(0, per_owner, unpack, 0)

    rows = lax.broadcasted_iota(jnp.int32, (8, cols), 0)

    def rim_copies(slot, up):
        side = 0 if up else 1
        peer = lax.max(me - 1, 0) if up else lax.min(me + 1, owners - 1)
        return pltpu.make_async_remote_copy(
            src_ref=rim_send.at[slot, side],
            dst_ref=rim_recv.at[slot, side],
            send_sem=rim_send_sem.at[slot, side],
            recv_sem=rim_recv_sem.at[slot, side],
            device_id={"blk": peer},
            device_id_type=pl.DeviceIdType.MESH,
        )

    def rim_start(slot):
        @pl.when(me > 0)
        def _():
            rim_copies(slot, True).start()

        @pl.when(me < owners - 1)
        def _():
            rim_copies(slot, False).start()

    def rim_wait(slot):
        @pl.when(me < owners - 1)
        def _():
            rim_copies(slot, True).wait_recv()

        @pl.when(me > 0)
        def _():
            rim_copies(slot, False).wait_recv()

    def rim_drain(slot):
        @pl.when(me > 0)
        def _():
            rim_copies(slot, True).wait_send()

        @pl.when(me < owners - 1)
        def _():
            rim_copies(slot, False).wait_send()

    def rim_tile(slot):
        return jnp.concatenate([rim_recv[slot, 0], rim_recv[slot, 1]], axis=0)

    def send_velocity(slot):
        rim_send[slot, 0, 0:2] = vel[0, 0:2]
        rim_send[slot, 0, 2:4] = vel[1, 0:2]
        rim_send[slot, 1, 0:2] = vel[1, 6:8]
        rim_send[slot, 1, 2:4] = vel[0, 6:8]
        rim_start(slot)

    def pick(tile, shift):
        return jnp.where(rows < 4, pltpu.roll(tile, 8 - shift, 0), pltpu.roll(tile, shift, 0))

    for f, (low, high) in enumerate(
        ((coef.at[0], coef.at[0]), *((stress_out.at[s], stress_out.at[s]) for s in range(3)))
    ):
        rim_send[ITERS, 0, f : f + 1] = low[0:1]
        rim_send[ITERS, 1, 3 - f : 4 - f] = high[7:8]
    rim_start(ITERS)
    send_velocity(0)
    rim_wait(ITERS)
    first = rim_tile(ITERS)
    edge[0] = first
    for s in range(3):
        edge[s + 1] = pick(first, s + 1)

    def east(a):
        return pltpu.roll(a, cols - 1, 1)

    def west(a):
        return pltpu.roll(a, 1, 1)

    def both_next(a, h):
        ra, rh = pltpu.roll(a, 7, 0), pltpu.roll(h, 7, 0)
        return jnp.where(rows == 7, rh, ra), jnp.where(rows == 7, ra, rh)

    def both_prev(a, h):
        ra, rh = pltpu.roll(a, 1, 0), pltpu.roll(h, 1, 0)
        return jnp.where(rows == 0, rh, ra), jnp.where(rows == 0, ra, rh)

    def stresses(vx, vy, nx, sx, ny, sy, p, m, xy, strength, mask):
        gux = 0.5 * (east(vx) - west(vx))
        gvx = 0.5 * (east(vy) - west(vy))
        gvy = 0.5 * (ny - sy)
        guy = 0.5 * (nx - sx)
        divergence = gux + gvy
        tension = gux - gvy
        shear = guy + gvx
        q = (
            divergence * divergence
            + (tension * tension + shear * shear) * EINV_SQ
            + DELTA_MIN_SQ
        )
        inv = lax.rsqrt(q)
        scaled = strength * inv
        half_mask = 0.5 * mask
        new_p = half_mask * (p + scaled * (divergence - q * inv))
        new_m = half_mask * (m + scaled * tension * EINV_SQ)
        new_xy = half_mask * (xy + scaled * shear * (0.5 * EINV_SQ))
        return new_p, new_m, new_xy

    def subcycle(t, _):
        rim_wait(t)
        vx, vy = vel[0], vel[1]
        hx = rim_tile(t)
        hy = pick(hx, 2)
        nx, hnx = both_next(vx, hx)
        sx, hsx = both_prev(vx, hx)
        ny, hny = both_next(vy, hy)
        sy, hsy = both_prev(vy, hy)
        mask = mask_buf[0]
        p, m, xy = stresses(
            vx, vy, nx, sx, ny, sy, stress_out[0], stress_out[1], stress_out[2], coef[0], mask
        )
        hp, hm, hxy = stresses(
            hx, hy, hnx, hsx, hny, hsy, edge[1], edge[2], edge[3], edge[0], mask_buf[1]
        )
        stress_out[0] = p
        stress_out[1] = m
        stress_out[2] = xy
        edge[1] = hp
        edge[2] = hm
        edge[3] = hxy
        sxx = 0.5 * (p + m)
        syy = 0.5 * (p - m)
        hyy = 0.5 * (hp - hm)
        force_x = 0.5 * (east(sxx) - west(sxx)) + 0.5 * (
            both_next(xy, hxy)[0] - both_prev(xy, hxy)[0]
        )
        force_y = 0.5 * (east(xy) - west(xy)) + 0.5 * (
            both_next(syy, hyy)[0] - both_prev(syy, hyy)[0]
        )
        mass, wx, wy, cx, cy = coef[1], coef[2], coef[3], coef[4], coef[5]
        rel_x = vx - cx
        rel_y = vy - cy
        q = rel_x * rel_x + rel_y * rel_y + SPEED_MIN_SQ
        drag = DRAG_COEFF * (q * lax.rsqrt(q))
        diag = mass + drag
        turning = CORIOLIS * mass
        rhs_x = mass * vx + force_x + wx + drag * cx
        rhs_y = mass * vy + force_y + wy + drag * cy
        inv_det = 1.0 / (diag * diag + turning * turning)
        vel[0] = mask * ((diag * rhs_x + turning * rhs_y) * inv_det) + (1.0 - mask) * cx
        vel[1] = mask * ((diag * rhs_y - turning * rhs_x) * inv_det) + (1.0 - mask) * cy

        @pl.when(t < ITERS - 1)
        def _():
            send_velocity(t + 1)

        return 0

    lax.fori_loop(0, ITERS, subcycle, 0)

    def to_blocks(j, _):
        at = pl.ds(pl.multiple_of(j * 128, 128), 128)
        vel_blocks[j, 0] = vel[0, :, at]
        vel_blocks[j, 1] = vel[1, :, at]
        return 0

    lax.fori_loop(0, per_owner, to_blocks, 0)

    def back_copy(peer):
        return pltpu.make_async_remote_copy(
            src_ref=back_buf.at[pl.ds(peer * cap, cap)],
            dst_ref=home_buf.at[pl.ds(me * cap, cap)],
            send_sem=back_send_sem.at[peer],
            recv_sem=back_recv_sem.at[me],
            device_id={"blk": peer},
            device_id_type=pl.DeviceIdType.MESH,
        )

    def home_copy(peer):
        return pltpu.make_async_remote_copy(
            src_ref=back_buf.at[pl.ds(me * cap, cap)],
            dst_ref=home_buf.at[pl.ds(peer * cap, cap)],
            send_sem=back_send_sem.at[me],
            recv_sem=back_recv_sem.at[peer],
            device_id={"blk": peer},
            device_id_type=pl.DeviceIdType.MESH,
        )

    def send_back(k, _):
        peer = lax.rem(me + k, owners)
        for r in range(cap):
            at = peer * cap + r
            back_buf[at] = vel_blocks[table[back_at + at]]
        back_copy(peer).start()
        return 0

    lax.fori_loop(half, owners, send_back, 0)
    lax.fori_loop(1, half, send_back, 0)
    for r in range(cap):
        at = me * cap + r
        home_buf[at] = vel_blocks[table[back_at + at]]

    def drain(k, _):
        out_copy(lax.rem(me + k, owners)).wait_send()
        return 0

    lax.fori_loop(1, owners, drain, 0)
    lax.fori_loop(0, ITERS + 1, lambda t, _: (rim_drain(t), 0)[1], 0)

    def came_home(k, _):
        home_copy(lax.rem(me + k, owners)).wait_recv()
        return 0

    lax.fori_loop(1, owners, came_home, 0)

    def place(slot, _):
        at = table[home_at + slot]
        block = home_buf[lax.max(at, 0)]
        held = jnp.full((8, 128), at, jnp.int32) >= 0
        vel_out[0, slot] = jnp.where(held, block[0], 0.0)
        vel_out[1, slot] = jnp.where(held, block[1], 0.0)
        return 0

    lax.fori_loop(0, slot_count, place, 0)

    def back_drain(k, _):
        back_copy(lax.rem(me + k, owners)).wait_send()
        return 0

    lax.fori_loop(1, owners, back_drain, 0)


def per_device(ocean_fields, stress_in, ocean_slot, ice_mask):
    owners = lax.axis_size("blk")
    my_index = lax.axis_index("blk")
    field_count, slot_count, block_rows, block_cols = ocean_fields.shape
    strip_cols = stress_in.shape[2]
    per_owner = strip_cols // block_cols
    pair_cap = 2 * per_owner // owners
    positions = owners * pair_cap
    table = index_tables(ocean_slot, owners, slot_count, per_owner, pair_cap, my_index)
    block = (block_rows, block_cols)
    strip = (block_rows, strip_cols)
    f32 = jnp.float32
    vmem = pl.BlockSpec(memory_space=pltpu.VMEM)
    smem = pl.BlockSpec(memory_space=pltpu.SMEM)
    return pl.pallas_call(
        functools.partial(kernel, owners, pair_cap, per_owner, slot_count),
        out_shape=(
            jax.ShapeDtypeStruct((2, slot_count) + block, f32),
            jax.ShapeDtypeStruct((3,) + strip, f32),
        ),
        in_specs=[smem, smem, vmem, vmem],
        out_specs=(vmem, vmem),
        scratch_shapes=[
            pltpu.VMEM((positions, field_count) + block, f32),
            pltpu.VMEM((positions, field_count) + block, f32),
            pltpu.VMEM((positions, 2) + block, f32),
            pltpu.VMEM((positions, 2) + block, f32),
            pltpu.VMEM((6,) + strip, f32),
            pltpu.VMEM((2,) + strip, f32),
            pltpu.VMEM((per_owner, 2) + block, f32),
            pltpu.VMEM((2,) + strip, f32),
            pltpu.VMEM((4,) + strip, f32),
            pltpu.VMEM((ITERS + 1, 2, 4, strip_cols), f32),
            pltpu.VMEM((ITERS + 1, 2, 4, strip_cols), f32),
            pltpu.SemaphoreType.DMA((owners,)),
            pltpu.SemaphoreType.DMA((owners,)),
            pltpu.SemaphoreType.DMA((owners,)),
            pltpu.SemaphoreType.DMA((owners,)),
            pltpu.SemaphoreType.DMA((ITERS + 1, 2)),
            pltpu.SemaphoreType.DMA((ITERS + 1, 2)),
        ],
        compiler_params=pltpu.CompilerParams(
            collective_id=0, has_side_effects=True, vmem_limit_bytes=40 * 1024 * 1024
        ),
    )(table, ice_mask, ocean_fields, stress_in)


def solution(mesh):
    placed = (P(None, ("groups", "blk"), None, None), P(None, ("groups", "blk"), None), P(), P())
    return jax.shard_map(
        per_device,
        mesh=mesh,
        in_specs=placed,
        out_specs=(P(None, ("groups", "blk"), None, None), P(None, ("groups", "blk"), None)),
        check_vma=False,
    )
```

time: 169 us -> 100 us (0.59)
  Pallas kernels: 0 us -> 92.4 us
  waiting for transfers between devices: 59 us -> 0 us
  starting transfers between devices: 58 us -> 0 us
  other arithmetic: 25.5 us -> 1.7 us
  local copies, waits for them, and re-layouts: 24.4 us -> 5.15 us
    pallas_call x0 -> x1, Pallas kernels: none -> 92.4 us  [per_device(): pl.pallas_call(functools.partial(kernel, owners, pair_cap, per_owner, slo...]
    all_to_all x2 -> x0, waiting for transfers between devices: 53.7 us -> none  [the longest x1 40.1 us: per_device(): lax.all_to_all(outgoing, 'blk', split_axis=1, concat_axis=1, tiled=True)]
    ppermute x8 -> x0, starting transfers between devices: 33.8 us -> none  [the longest x4 28.5 us: extended_2(): lax.ppermute(lax.slice_in_dim(block, block.shape[dim] - width, None, axis...]
    all_to_all x2 -> x0, starting transfers between devices: 24.2 us -> none  [the longest x1 16.7 us: per_device(): lax.all_to_all(back_send, 'blk', split_axis=1, concat_axis=1, tiled=True)]
    mul x24 -> x0, other arithmetic: 9.45 us -> none  [the longest x7 3.18 us: momentum_section(): new_x = (cell_mask * solved_x + (1.0 - cell_mask) * current_x) * row_valid]
    concatenate x85 -> x0, local copies, waits for them, and re-layouts: 8.39 us -> none  [the longest x48 5 us: column_next(): return jnp.roll(values, -1, axis=1)]
    scatter x4 -> x0, local copies, waits for them, and re-layouts: 7.93 us -> none  [the longest x1 2.78 us: per_device(): velocity_out = jnp.zeros((2, slot_count + 1, block_rows, block_cols), jnp...]
    select_n x8 -> x0, other arithmetic: 5.25 us -> none  [the longest x1 3.09 us: per_device(): outgoing = jnp.take(padded, send_index, axis=1)]
  transfers between devices with their start and end apart: 10 -> 0, of which waited for: 5 -> 0; matrix products, arithmetic and copies ran while one was open for 2% -> 0% of each run, Pallas kernels for 0% -> 0%
where the time goes in v1:
time: 100 us
  Pallas kernels  92.4 us (92%)
  local copies, waits for them, and re-layouts  5.15 us (5%)
  other arithmetic  1.7 us (2%)
    pallas_call x1, Pallas kernels, per_device(): pl.pallas_call(functools.partial(kernel, owners, pair_cap, per_owner, slo...  92.4 us
    unnamed x8, local copies, waits for them, and re-layouts  4.82 us

profile of v1, /device:TPU:0, one launch (start us, length us, event | category | flops | bytes accessed | tf_op | source)
XLA Modules:
  0.0 100.0 jit_solution(16454406285290900359)
XLA Ops:
  0.7 0.7 fusion.1
  1.4 0.1 add.49
  1.4 0.1 reshape.55
  1.5 0.2 select_reduce_fusion.4
  1.7 0.1 select_reduce_fusion.3
  1.8 0.3 select_reduce_fusion
  2.2 0.1 select_reduce_fusion.2
  2.4 0.1 copy.6
  2.4 0.1 sub.18
  2.5 0.1 select_reduce_fusion.1
  2.7 0.1 pad_add_fusion.table
  2.7 0.0 copy-start
  2.7 1.6 %copy-done = f32[8,64,8,128]{3,2,1,0:T(8,128)S(1)} copy-done((f32[8,64,8,128]{3,2,1,0:T(8,128)S(1)}, f32[8,64,8,128]{3,2,1,0:T(8,128)}, u32[]{:S(2)}) %copy-start) | copy-done | bytes 2097176
  4.3 0.0 copy-start.1
  4.3 1.0 copy-done.1
  5.3 0.0 copy-start.2
  5.3 0.7 copy-done.2
  6.0 92.4 %shard_map.59 = (f32[2,64,8,128]{3,2,1,0:T(8,128)S(1)}, f32[3,8,4096]{2,1,0:T(8,128)S(1)}) custom-call(s32[224]{0:T(256)S(1)} %pad_add_fusion.table, s32[512]{0:T(512)S(1)} %copy-done.2, f32[8,64,8,128]{3,2,1,0:T(8,128)S(1)} %copy-done, f32[3,8,4096]{2,1,0:T(8,128)S(1)} %copy-done.1), custom_call_target="tpu_custom_call" | custom-call | tf_op jit(solution)/shard_map/pallas_call | solution.py:376
  98.4 0.8 copy.9
  99.2 0.7 copy.10
  (8 shorter events, 0.1 us)
Async XLA Ops:
  2.7 1.6 %copy-start = (f32[8,64,8,128]{3,2,1,0:T(8,128)S(1)}, f32[8,64,8,128]{3,2,1,0:T(8,128)}, u32[]{:S(2)}) copy-start(f32[8,64,8,128]{3,2,1,0:T(8,128)} %ocean.1) | copy-start | bytes 6291460
  4.3 1.0 copy-start.1
  5.3 0.7 copy-start.2

commit v2 on v1

v2 whole, which is shorter than its diff:
```python
import functools

import jax
import jax.numpy as jnp
from jax import lax
from jax.experimental import pallas as pl
from jax.experimental.pallas import tpu as pltpu
from jax.sharding import PartitionSpec as P

ITERS = 6
EINV_SQ = 0.25
DELTA_MIN_SQ = 0.01
DRAG_COEFF = 0.5
CORIOLIS = 0.5
SPEED_MIN_SQ = 0.0025


def index_tables(ocean_slot, owners, slot_count, per_owner, pair_cap, my_index):
    source = (ocean_slot // slot_count).reshape(owners, per_owner)
    place = (ocean_slot % slot_count).reshape(owners, per_owner)
    buffer_slots = owners * pair_cap
    earlier = jnp.arange(per_owner)[None, :] < jnp.arange(per_owner)[:, None]
    is_mine = source == my_index
    rank = jnp.sum(jnp.where(is_mine[:, None, :] & earlier[None], 1, 0), axis=2)
    hit = is_mine[:, :, None] & (rank[:, :, None] == jnp.arange(pair_cap)[None, None, :])
    send_index = (jnp.sum(jnp.where(hit, place[:, :, None] + 1, 0), axis=1) - 1).reshape(-1)
    slots = jnp.arange(slot_count)
    match = send_index[None, :] == slots[:, None]
    home_index = jnp.sum(jnp.where(match, jnp.arange(buffer_slots)[None, :] + 1, 0), axis=1) - 1
    mine = lax.dynamic_slice_in_dim(source, my_index, 1, 0)[0]
    my_rank = jnp.sum(jnp.where((mine[None, :] == mine[:, None]) & earlier, 1, 0), axis=1)
    receive_index = mine * pair_cap + my_rank
    back = receive_index[None, :] == jnp.arange(buffer_slots)[:, None]
    back_index = jnp.sum(jnp.where(back, jnp.arange(per_owner)[None, :], 0), axis=1)
    return jnp.concatenate(
        [jnp.maximum(send_index, 0), home_index, receive_index, back_index]
    ).astype(jnp.int32)


def kernel(
    owners, pair_cap, per_owner, slot_count,
    table, mask_ref, ocean_hbm, stress_in, vel_out, stress_out,
    ocean, send_a, send_b, recv_a, recv_b, back_buf, home_buf, coef, vel, vel_blocks, mask_buf, edge, solve,
    rim_send, rim_recv,
    load_sem, send_sem, recv_sem, back_send_sem, back_recv_sem, rim_send_sem, rim_recv_sem,
):
    me = lax.axis_index("blk")
    cap = pair_cap
    home_at = owners * cap
    receive_at = home_at + slot_count
    back_at = receive_at + per_owner
    cols = stress_in.shape[2]
    first_count = send_a.shape[1]

    load_ocean = pltpu.make_async_copy(ocean_hbm, ocean, load_sem.at[0])
    load_stress = pltpu.make_async_copy(stress_in, stress_out, load_sem.at[1])
    load_ocean.start()
    load_stress.start()
    rim_recv[...] = jnp.zeros_like(rim_recv)
    barrier = pltpu.get_barrier_semaphore()

    def greet(k, _):
        pl.semaphore_signal(
            barrier, inc=1, device_id={"blk": lax.rem(me + k, owners)},
            device_id_type=pl.DeviceIdType.MESH,
        )
        return 0

    lax.fori_loop(1, owners, greet, 0)

    row = lax.broadcasted_iota(jnp.int32, (8, 128), 0)
    above = lax.max(me - 1, 0)
    below = lax.min(me + 1, owners - 1)
    above_ok = jnp.where(me > 0, 1.0, 0.0)
    below_ok = jnp.where(me < owners - 1, 1.0, 0.0)

    def mask_block(j, _):
        at = pl.ds(pl.multiple_of(j * 128, 128), 128)
        own = mask_ref[me * per_owner + j].astype(jnp.float32)
        mask_buf[0, :, at] = jnp.full((8, 128), own)
        low = mask_ref[below * per_owner + j].astype(jnp.float32) * below_ok
        high = mask_ref[above * per_owner + j].astype(jnp.float32) * above_ok
        mask_buf[1, :, at] = jnp.where(row < 2, high, jnp.where(row < 6, own, low))
        return 0

    lax.fori_loop(0, per_owner, mask_block, 0)
    load_ocean.wait()
    pl.semaphore_wait(barrier, owners - 1)

    def pair_copy(part, source, dest):
        src, dst = (send_a, recv_a) if part == 0 else (send_b, recv_b)
        return pltpu.make_async_remote_copy(
            src_ref=src.at[pl.ds(dest * cap, cap)],
            dst_ref=dst.at[pl.ds(source * cap, cap)],
            send_sem=send_sem.at[part, dest],
            recv_sem=recv_sem.at[part, source],
            device_id={"blk": lax.rem(dest + source - me + owners, owners)},
            device_id_type=pl.DeviceIdType.MESH,
        )

    def send_first(k, _):
        peer = lax.rem(me + k, owners)
        for r in range(cap):
            at = peer * cap + r
            send_a[at] = ocean[0:first_count, table[at]]
        pair_copy(0, me, peer).start()
        return 0

    def send_second(k, _):
        peer = lax.rem(me + k, owners)
        for r in range(cap):
            at = peer * cap + r
            send_b[at] = ocean[first_count:, table[at]]
        pair_copy(1, me, peer).start()
        return 0

    half = owners // 2
    for send in (send_first, send_second):
        lax.fori_loop(half, owners, send, 0)
        lax.fori_loop(1, half, send, 0)
    for r in range(cap):
        at = me * cap + r
        recv_a[at] = ocean[0:first_count, table[at]]
        recv_b[at] = ocean[first_count:, table[at]]
    load_stress.wait()

    def wait_first(k, _):
        pair_copy(0, lax.rem(me + k, owners), me).wait_recv()
        return 0

    def wait_second(k, _):
        pair_copy(1, lax.rem(me + k, owners), me).wait_recv()
        return 0

    def unpack_first(j, _):
        at = pl.ds(pl.multiple_of(j * 128, 128), 128)
        block = recv_a[table[receive_at + j]]
        vel[0, :, at] = block[0]
        vel[1, :, at] = block[1]
        coef[0, :, at] = block[2]
        return 0

    def unpack_second(j, _):
        at = pl.ds(pl.multiple_of(j * 128, 128), 128)
        block = recv_b[table[receive_at + j]]
        for f in range(5):
            coef[1 + f, :, at] = block[f]
        return 0

    lax.fori_loop(1, owners, wait_first, 0)
    lax.fori_loop(0, per_owner, unpack_first, 0)

    rows = lax.broadcasted_iota(jnp.int32, (8, cols), 0)

    def rim_copy(slot, side):
        peer = above if side == 0 else below
        return pltpu.make_async_remote_copy(
            src_ref=rim_send.at[slot, side],
            dst_ref=rim_recv.at[slot, side],
            send_sem=rim_send_sem.at[slot, side],
            recv_sem=rim_recv_sem.at[slot, side],
            device_id={"blk": peer},
            device_id_type=pl.DeviceIdType.MESH,
        )

    def rim_start(slot):
        @pl.when(me > 0)
        def _():
            rim_copy(slot, 0).start()

        @pl.when(me < owners - 1)
        def _():
            rim_copy(slot, 1).start()

    def rim_wait(slot):
        @pl.when(me < owners - 1)
        def _():
            rim_copy(slot, 0).wait_recv()

        @pl.when(me > 0)
        def _():
            rim_copy(slot, 1).wait_recv()

    def rim_drain(slot):
        @pl.when(me > 0)
        def _():
            rim_copy(slot, 0).wait_send()

        @pl.when(me < owners - 1)
        def _():
            rim_copy(slot, 1).wait_send()

    def rim_tile(slot):
        return jnp.concatenate([rim_recv[slot, 1], rim_recv[slot, 0]], axis=0)

    def send_velocity(slot):
        rim_send[slot, 0, 0:2] = vel[1, 0:2]
        rim_send[slot, 0, 2:4] = vel[0, 0:2]
        rim_send[slot, 1, 0:2] = vel[0, 6:8]
        rim_send[slot, 1, 2:4] = vel[1, 6:8]
        rim_start(slot)

    def turn(tile, shift):
        return pltpu.roll(tile, shift % 8, 0) if shift % 8 else tile

    def halves(tile, upper, lower):
        return jnp.where(rows < 4, turn(tile, upper), turn(tile, lower))

    def packed(own, rim):
        return jnp.where((rows >= 2) & (rows < 6), halves(own, 2, -2), rim)

    for f, field in enumerate((coef.at[0], *(stress_out.at[s] for s in range(3)))):
        rim_send[ITERS, 0, 3 - f : 4 - f] = field[0:1]
        rim_send[ITERS, 1, f : f + 1] = field[7:8]
    rim_start(ITERS)
    send_velocity(0)
    rim_wait(ITERS)
    first = rim_tile(ITERS)
    for f, field in enumerate((coef.at[0], *(stress_out.at[s] for s in range(3)))):
        edge[f] = packed(field[...], halves(first, 1 - f, f - 1))

    def east(a):
        return pltpu.roll(a, cols - 1, 1)

    def west(a):
        return pltpu.roll(a, 1, 1)

    def stresses(vx, vy, p, m, xy, strength, mask):
        gux = 0.5 * (east(vx) - west(vx))
        gvx = 0.5 * (east(vy) - west(vy))
        gvy = 0.5 * (turn(vy, -1) - turn(vy, 1))
        guy = 0.5 * (turn(vx, -1) - turn(vx, 1))
        divergence = gux + gvy
        tension = gux - gvy
        shear = guy + gvx
        q = (
            divergence * divergence
            + (tension * tension + shear * shear) * EINV_SQ
            + DELTA_MIN_SQ
        )
        inv = lax.rsqrt(q)
        scaled = strength * inv
        half_mask = 0.5 * mask
        new_p = half_mask * (p + scaled * (divergence - q * inv))
        new_m = half_mask * (m + scaled * tension * EINV_SQ)
        new_xy = half_mask * (xy + scaled * shear * (0.5 * EINV_SQ))
        return new_p, new_m, new_xy

    def prepare():
        vx, vy, mask = vel[0], vel[1], mask_buf[0]
        mass, wx, wy, cx, cy = coef[1], coef[2], coef[3], coef[4], coef[5]
        rel_x = vx - cx
        rel_y = vy - cy
        q = rel_x * rel_x + rel_y * rel_y + SPEED_MIN_SQ
        drag = DRAG_COEFF * (q * lax.rsqrt(q))
        diag = mass + drag
        turning = CORIOLIS * mass
        base_x = mass * vx + wx + drag * cx
        base_y = mass * vy + wy + drag * cy
        inv_det = mask / (diag * diag + turning * turning)
        along = diag * inv_det
        across = turning * inv_det
        solve[0] = along
        solve[1] = across
        solve[2] = along * base_x + across * base_y + (1.0 - mask) * cx
        solve[3] = along * base_y - across * base_x + (1.0 - mask) * cy

    def subcycle(t, _):
        inner = stresses(
            vel[0], vel[1], stress_out[0], stress_out[1], stress_out[2], coef[0], mask_buf[0]
        )
        for s in range(3):
            stress_out[s] = inner[s]

        @pl.when(t > 0)
        def _():
            prepare()

        rim_wait(t)
        rim = rim_tile(t)
        outer = stresses(
            packed(vel[0], rim),
            packed(vel[1], halves(rim, -2, 2)),
            edge[1], edge[2], edge[3], edge[0], mask_buf[1],
        )
        for s in range(3):
            edge[s + 1] = outer[s]
            stress_out[s] = jnp.where(
                rows == 0, turn(outer[s], -2), jnp.where(rows == 7, turn(outer[s], 2), stress_out[s])
            )

        @pl.when(t == 0)
        def _():
            lax.fori_loop(1, owners, wait_second, 0)
            lax.fori_loop(0, per_owner, unpack_second, 0)
            prepare()

        def across_rows(own, beside):
            above_it = jnp.where(rows == 7, turn(beside, 1), turn(own, -1))
            below_it = jnp.where(rows == 0, turn(beside, -1), turn(own, 1))
            return above_it - below_it

        p, m, xy = stress_out[0], stress_out[1], stress_out[2]
        sxx = 0.5 * (p + m)
        syy = 0.5 * (p - m)
        beside_yy = 0.5 * (edge[1] - edge[2])
        force_x = 0.5 * (east(sxx) - west(sxx)) + 0.5 * across_rows(xy, edge[3])
        force_y = 0.5 * (east(xy) - west(xy)) + 0.5 * across_rows(syy, beside_yy)
        vel[0] = solve[0] * force_x + solve[1] * force_y + solve[2]
        vel[1] = solve[0] * force_y - solve[1] * force_x + solve[3]

        @pl.when(t < ITERS - 1)
        def _():
            send_velocity(t + 1)

        return 0

    lax.fori_loop(0, ITERS, subcycle, 0)

    def to_blocks(j, _):
        at = pl.ds(pl.multiple_of(j * 128, 128), 128)
        vel_blocks[j, 0] = vel[0, :, at]
        vel_blocks[j, 1] = vel[1, :, at]
        return 0

    lax.fori_loop(0, per_owner, to_blocks, 0)

    def back_copy(source, dest):
        return pltpu.make_async_remote_copy(
            src_ref=back_buf.at[pl.ds(dest * cap, cap)],
            dst_ref=home_buf.at[pl.ds(source * cap, cap)],
            send_sem=back_send_sem.at[dest],
            recv_sem=back_recv_sem.at[source],
            device_id={"blk": lax.rem(dest + source - me + owners, owners)},
            device_id_type=pl.DeviceIdType.MESH,
        )

    def send_back(k, _):
        peer = lax.rem(me + k, owners)
        for r in range(cap):
            at = peer * cap + r
            back_buf[at] = vel_blocks[table[back_at + at]]
        back_copy(me, peer).start()
        return 0

    lax.fori_loop(half, owners, send_back, 0)
    lax.fori_loop(1, half, send_back, 0)
    for r in range(cap):
        at = me * cap + r
        home_buf[at] = vel_blocks[table[back_at + at]]

    def drain(k, _):
        pair_copy(0, me, lax.rem(me + k, owners)).wait_send()
        pair_copy(1, me, lax.rem(me + k, owners)).wait_send()
        return 0

    lax.fori_loop(1, owners, drain, 0)
    lax.fori_loop(0, ITERS + 1, lambda t, _: (rim_drain(t), 0)[1], 0)

    def came_home(k, _):
        back_copy(lax.rem(me + k, owners), me).wait_recv()
        return 0

    lax.fori_loop(1, owners, came_home, 0)

    def place(slot, _):
        at = table[home_at + slot]
        block = home_buf[lax.max(at, 0)]
        held = jnp.full((8, 128), at, jnp.int32) >= 0
        vel_out[0, slot] = jnp.where(held, block[0], 0.0)
        vel_out[1, slot] = jnp.where(held, block[1], 0.0)
        return 0

    lax.fori_loop(0, slot_count, place, 0)

    def back_drain(k, _):
        back_copy(me, lax.rem(me + k, owners)).wait_send()
        return 0

    lax.fori_loop(1, owners, back_drain, 0)


def per_device(ocean_fields, stress_in, ocean_slot, ice_mask):
    owners = lax.axis_size("blk")
    my_index = lax.axis_index("blk")
    field_count, slot_count, block_rows, block_cols = ocean_fields.shape
    strip_cols = stress_in.shape[2]
    per_owner = strip_cols // block_cols
    pair_cap = 2 * per_owner // owners
    positions = owners * pair_cap
    table = index_tables(ocean_slot, owners, slot_count, per_owner, pair_cap, my_index)
    block = (block_rows, block_cols)
    strip = (block_rows, strip_cols)
    f32 = jnp.float32
    vmem = pl.BlockSpec(memory_space=pltpu.VMEM)
    smem = pl.BlockSpec(memory_space=pltpu.SMEM)
    anywhere = pl.BlockSpec(memory_space=pl.ANY)
    first_count = 3
    rest_count = field_count - first_count
    return pl.pallas_call(
        functools.partial(kernel, owners, pair_cap, per_owner, slot_count),
        out_shape=(
            jax.ShapeDtypeStruct((2, slot_count) + block, f32),
            jax.ShapeDtypeStruct((3,) + strip, f32),
        ),
        in_specs=[smem, smem, anywhere, anywhere],
        out_specs=(vmem, vmem),
        scratch_shapes=[
            pltpu.VMEM((field_count, slot_count) + block, f32),
            pltpu.VMEM((positions, first_count) + block, f32),
            pltpu.VMEM((positions, rest_count) + block, f32),
            pltpu.VMEM((positions, first_count) + block, f32),
            pltpu.VMEM((positions, rest_count) + block, f32),
            pltpu.VMEM((positions, 2) + block, f32),
            pltpu.VMEM((positions, 2) + block, f32),
            pltpu.VMEM((6,) + strip, f32),
            pltpu.VMEM((2,) + strip, f32),
            pltpu.VMEM((per_owner, 2) + block, f32),
            pltpu.VMEM((2,) + strip, f32),
            pltpu.VMEM((4,) + strip, f32),
            pltpu.VMEM((4,) + strip, f32),
            pltpu.VMEM((ITERS + 1, 2, 4, strip_cols), f32),
            pltpu.VMEM((ITERS + 1, 2, 4, strip_cols), f32),
            pltpu.SemaphoreType.DMA((2,)),
            pltpu.SemaphoreType.DMA((2, owners)),
            pltpu.SemaphoreType.DMA((2, owners)),
            pltpu.SemaphoreType.DMA((owners,)),
            pltpu.SemaphoreType.DMA((owners,)),
            pltpu.SemaphoreType.DMA((ITERS + 1, 2)),
            pltpu.SemaphoreType.DMA((ITERS + 1, 2)),
        ],
        compiler_params=pltpu.CompilerParams(
            collective_id=0, has_side_effects=True, vmem_limit_bytes=40 * 1024 * 1024
        ),
    )(table, ice_mask, ocean_fields, stress_in)


def solution(mesh):
    placed = (P(None, ("groups", "blk"), None, None), P(None, ("groups", "blk"), None), P(), P())
    return jax.shard_map(
        per_device,
        mesh=mesh,
        in_specs=placed,
        out_specs=(P(None, ("groups", "blk"), None, None), P(None, ("groups", "blk"), None)),
        check_vma=False,
    )
```

time: 100 us -> 95.4 us (0.954)
  Pallas kernels: 92.4 us -> 87.6 us
    pallas_call x1, Pallas kernels: 92.4 us -> 87.6 us  [per_device(): pl.pallas_call(functools.partial(kernel, owners, pair_cap, per_owner, slo...]
where the time goes in v2:
time: 95.4 us; the launch traced here: 95.1 us
  Pallas kernels  87.6 us (92%)
  local copies, waits for them, and re-layouts  5.15 us (5%)
  other arithmetic  1.7 us (2%)
    pallas_call x1, Pallas kernels, per_device(): pl.pallas_call(functools.partial(kernel, owners, pair_cap, per_owner, slo...  87.6 us
    unnamed x8, local copies, waits for them, and re-layouts  4.82 us

profile of v2, /device:TPU:0, one launch (start us, length us, event | category | flops | bytes accessed | tf_op | source)
XLA Modules:
  0.0 95.1 jit_solution(2974272733887075023)
XLA Ops:
  0.7 0.7 fusion.1
  1.4 0.1 add.49
  1.4 0.1 reshape.55
  1.5 0.2 select_reduce_fusion.4
  1.7 0.1 select_reduce_fusion.3
  1.8 0.3 select_reduce_fusion
  2.2 0.1 select_reduce_fusion.2
  2.4 0.1 copy.6
  2.4 0.1 sub.18
  2.5 0.1 select_reduce_fusion.1
  2.7 0.1 pad_add_fusion.table
  2.7 0.0 copy-start
  2.7 1.6 %copy-done = f32[8,64,8,128]{3,2,1,0:T(8,128)S(1)} copy-done((f32[8,64,8,128]{3,2,1,0:T(8,128)S(1)}, f32[8,64,8,128]{3,2,1,0:T(8,128)}, u32[]{:S(2)}) %copy-start) | copy-done | bytes 2097176
  4.3 0.0 copy-start.1
  4.3 1.0 %copy-done.1 = f32[3,8,4096]{2,1,0:T(8,128)S(1)} copy-done((f32[3,8,4096]{2,1,0:T(8,128)S(1)}, f32[3,8,4096]{2,1,0:T(8,128)}, u32[]{:S(2)}) %copy-start.1) | copy-done | bytes 393240
  5.3 0.0 copy-start.2
  5.3 0.7 copy-done.2
  6.0 87.6 %shard_map.59 = (f32[2,64,8,128]{3,2,1,0:T(8,128)S(1)}, f32[3,8,4096]{2,1,0:T(8,128)S(1)}) custom-call(s32[224]{0:T(256)S(1)} %pad_add_fusion.table, s32[512]{0:T(512)S(1)} %copy-done.2, f32[8,64,8,128]{3,2,1,0:T(8,128)S(1)} %copy-done, f32[3,8,4096]{2,1,0:T(8,128)S(1)} %copy-done.1), custom_call_target="tpu_custom_call" | custom-call | tf_op jit(solution)/shard_map/pallas_call | solution.py:400
  93.6 0.8 copy.9
  94.4 0.7 copy.10
  (8 shorter events, 0.1 us)
Async XLA Ops:
  2.7 1.6 %copy-start = (f32[8,64,8,128]{3,2,1,0:T(8,128)S(1)}, f32[8,64,8,128]{3,2,1,0:T(8,128)}, u32[]{:S(2)}) copy-start(f32[8,64,8,128]{3,2,1,0:T(8,128)} %ocean_hbm.1) | copy-start | bytes 6291460
  4.3 1.0 %copy-start.1 = (f32[3,8,4096]{2,1,0:T(8,128)S(1)}, f32[3,8,4096]{2,1,0:T(8,128)}, u32[]{:S(2)}) copy-start(f32[3,8,4096]{2,1,0:T(8,128)} %stress_in.1) | copy-start | bytes 1179652
  5.3 0.7 copy-start.2
